TPU v7x, 32 devices: a whole 2x2x4 slice. The times are simulated.
32 devices in a mesh: groups: 2 (over x), corpus: 8 (over z, y), retrieve: 2 (over core).
Axes of the slice: x: 2, y: 2, z: 4, core: 2. Of those that a mesh axis runs over, the one named last changes fastest.
Arguments:
- weights: int32 [4], replicated, may hold values from 1 to 16
- q_wide: bfloat16 [2, 256, 4096], P('retrieve', ('groups', 'corpus')), parts along dimension 1
- q_mid: bfloat16 [256, 3584], P(('groups', 'corpus'), 'retrieve'), parts along dimension 0
- q_narrow: bfloat16 [256, 1024], P(('groups', 'corpus'), 'retrieve'), parts along dimension 0
- pass_wide: bfloat16 [2, 12288, 4096], P('retrieve', ('groups', 'corpus')), parts along dimension 1
- pass_mid: bfloat16 [12288, 3584], P(('groups', 'corpus'), 'retrieve'), parts along dimension 0
- pass_narrow: bfloat16 [12288, 1024], P(('groups', 'corpus'), 'retrieve'), parts along dimension 0
Outputs:
- united: float32 [128, 12288], P('retrieve', ('groups', 'corpus')), parts along dimension 1
There are 2 independent parts, one for each index of `groups`. A program takes and returns all parts, laid end to end along the dimension named above; an argument that names none is the same for every part. Nothing has to cross between parts.
Inputs may be any that keep to these rules, and one draw needn't show every extreme that they name: `weights`: numerators over a fixed denominator of 16.
All inputs are finite; a program needn't handle non-finite values.
Results may differ from a plain program's by a relative error of at most 0.0003.
Values may be sent and summed in bfloat16 or wider, within the bound.
A program may use at most 128 MiB of HBM per device.

v0:
```python
import math

import jax
import jax.numpy as jnp
from jax import lax
from jax.sharding import PartitionSpec as P

WIDE = 4096
MID = 3584
NARROW = 1024


unite_scale = 1.0 / 16.0


def normalise(wide_score, mid_score, narrow_score, slab_size):
    peak_rows = lax.pmax(
        (jnp.max(wide_score, axis=1), jnp.max(mid_score, axis=1), jnp.max(narrow_score, axis=1)),
        "corpus",
    )
    powers = [
        jnp.exp(score_part - peak_part[:, None])
        for score_part, peak_part in zip((wide_score, mid_score, narrow_score), peak_rows)
    ]
    totals = lax.psum(
        (jnp.sum(powers[0], axis=1), jnp.sum(powers[1], axis=1), jnp.sum(powers[2], axis=1)),
        "corpus",
    )
    return [
        power_part * (slab_size / total_part)[:, None]
        for power_part, total_part in zip(powers, totals)
    ]


def reduce_rows(tile):
    return lax.psum_scatter(tile, "retrieve", scatter_dimension=0, tiled=True)


def body(weights, q_wide, q_mid, q_narrow, pass_wide, pass_mid, pass_narrow):
    wide_cols = q_wide.shape[2]
    mid_cols = q_mid.shape[1]
    wide_rows = pass_wide[0]
    core_index = lax.axis_index("retrieve")
    queries = jnp.concatenate([q_wide[0], q_mid, q_narrow], axis=1)
    piece = lax.all_gather(queries, "corpus", axis=0, tiled=True)
    wide_part = jnp.einsum(
        "qd,pd->qp", piece[:, :wide_cols], wide_rows, preferred_element_type=jnp.float32
    )
    mid_part = jnp.einsum(
        "qd,pd->qp",
        piece[:, wide_cols : wide_cols + mid_cols],
        pass_mid,
        preferred_element_type=jnp.float32,
    )
    narrow_part = jnp.einsum(
        "qd,pd->qp",
        piece[:, wide_cols + mid_cols :],
        pass_narrow,
        preferred_element_type=jnp.float32,
    )
    scores = jnp.stack([wide_part, mid_part, narrow_part], axis=0)
    slab_size = float(pass_wide.shape[1] * lax.axis_size("corpus"))
    uniting = weights.astype(jnp.float32) * unite_scale
    own_weight = jnp.sum(jnp.where(jnp.arange(2) == core_index, uniting[:2], 0.0))
    wide_score = scores[0] * (1.0 / math.sqrt(WIDE))
    joined = lax.psum(scores[1:], "retrieve")
    probs = normalise(
        wide_score,
        joined[0] * (1.0 / math.sqrt(MID)),
        joined[1] * (1.0 / math.sqrt(NARROW)),
        slab_size,
    )
    tile = own_weight * probs[0] + 0.5 * (uniting[2] * probs[1] + uniting[3] * probs[2])
    return reduce_rows(tile)


def solution(mesh):
    return jax.shard_map(
        body,
        mesh=mesh,
        in_specs=(
            P(),
            P("retrieve", ("groups", "corpus"), None),
            P(("groups", "corpus"), "retrieve"),
            P(("groups", "corpus"), "retrieve"),
            P("retrieve", ("groups", "corpus"), None),
            P(("groups", "corpus"), "retrieve"),
            P(("groups", "corpus"), "retrieve"),
        ),
        out_specs=P("retrieve", ("groups", "corpus")),
        check_vma=False,
    )
```

profile of v0, /device:TPU:0, one launch (start us, length us, event | category | flops | bytes accessed | tf_op | source)
XLA Modules:
  0.0 138.4 jit_solution(9043413787728045229)
XLA Ops:
  6.5 0.0 copy-start
  6.5 0.0 all-gather.2.cloned.1.call-start
  6.5 1.8 %pad_maximum_fusion.1 = bf16[16,6400]{1,0:T(8,128)(2,1)} fusion(bf16[16,512]{1,0:T(8,128)(2,1)} %param.10, bf16[16,1792]{1,0:T(8,128)(2,1)} %param.9, bf16[16,4096]{1,0:T(8,128)(2,1)} %bitcast.32), kind=kLoop, calls=%fused_computation.21 | loop fusion | flops 614400 | bytes 409600 | tf_op jit(solution)/shard_map/concatenate | solution.py:44
  8.3 0.0 all-gather.2.cloned.1.call-update
  8.4 0.0 all-reduce.4.cloned.1.call-start
  8.4 48.4 %all-gather.2.cloned.1.call-done = bf16[128,6400]{1,0:T(8,128)(2,1)} async-done(((bf16[16,6400]{1,0:T(8,128)(2,1)}), bf16[128,6400]{1,0:T(8,128)(2,1)}) %all-gather.2.cloned.1.call-update) | async-done | bytes 1638416 | tf_op jit(solution)/shard_map/all_gather | solution.py:45
  56.8 1.6 %convolution_bitcast_fusion.1 = f32[1,128,768]{2,1,0:T(8,128)S(1)} fusion(bf16[768,512]{1,0:T(8,128)(2,1)} %param.13, bf16[128,6400]{1,0:T(8,128)(2,1)} %all-gather.2.cloned.1.call-done), kind=kOutput, calls=%fused_computation.3 | convolution fusion | flops 100663296 | bytes 1310720 | tf_op jit(solution)/shard_map/qd,pd->qp/dot_general | solution.py:55
  58.4 0.0 copy-done
  58.4 0.0 copy-start.1
  58.4 2.1 %convolution_bitcast_fusion = f32[1,128,768]{2,1,0:T(8,128)S(1)} fusion(bf16[768,1792]{1,0:T(8,128)(2,1)S(1)} %copy-done, bf16[128,6400]{1,0:T(8,128)(2,1)} %all-gather.2.cloned.1.call-done), kind=kOutput, calls=%fused_computation.2 | convolution fusion | flops 352321536 | bytes 3604480 | tf_op jit(solution)/shard_map/qd,pd->qp/dot_general | solution.py:49
  60.5 0.9 pad_maximum_fusion
  61.4 0.0 all-reduce.4.cloned.1.call-update
  61.5 0.0 reduce-scatter.2.cloned.1.call-start
  61.5 0.0 copy-done.1
  61.5 0.6 fusion.16
  62.1 0.7 fusion.15
  62.8 5.4 %fusion.17 = (f32[128]{0:T(128)S(1)}, f32[128,768]{1,0:T(8,128)S(1)}) fusion(bf16[1,768,4096]{2,1,0:T(8,128)(2,1)} %param.11, bf16[128,6400]{1,0:T(8,128)(2,1)} %all-gather.2.cloned.1.call-done), kind=kOutput, calls=%fused_computation.30 | convolution fusion | flops 805502848 | bytes 7733760 | tf_op jit(solution)/shard_map/qd,pd->qp/dot_general | solution.py:46
  68.2 11.6 %all-reduce.4.cloned.1.call-done = f32[2,128,768]{2,1,0:T(8,128)} async-done(((f32[2,128,768]{2,1,0:T(8,128)}), f32[2,128,768]{2,1,0:T(8,128)}) %all-reduce.4.cloned.1.call-update) | async-done | bytes 786448 | tf_op jit(solution)/shard_map/psum | solution.py:66
  79.8 1.2 fusion.12
  81.0 21.6 %all-reduce.1 = (f32[128]{0:T(128)S(1)}, f32[128]{0:T(128)S(1)}, f32[128]{0:T(128)S(1)}) all-reduce(f32[128]{0:T(128)S(1)} %get-tuple-element.7, f32[128]{0:T(128)S(1)} %get-tuple-element.8, f32[128]{0:T(128)S(1)} %get-tuple-element.17), channel_id=1, replica_groups=mesh['groups'=2,'corpus'=8,'retrieve'=2] {'corpus'}, use_global_device_ids=true, to_apply=%region_7.8 | all-reduce | flops 384 | bytes 3072 | tf_op jit(solution)/shard_map/pmax | solution.py:17
  102.6 1.4 %fusion.10 = (f32[128]{0:T(128)S(1)}, f32[128]{0:T(128)S(1)}, f32[128]{0:T(128)S(1)}) fusion(f32[2,128,768]{2,1,0:T(8,128)} %all-reduce.4.cloned.1.call-done, f32[128]{0:T(128)S(1)} %get-tuple-element.12, f32[128]{0:T(128)S(1)} %get-tuple-element.13, f32[128,768]{1,0:T(8,128)S(1)} %get-tuple-element.18, f32[128]{0:T(128)S(1)} %get-tuple-element.14), kind=kLoop, calls=%fused_computation.17 | loop fusion | flops 786048 | bytes 1182720 | tf_op jit(solution)/shard_map/reduce_sum | solution.py:26
  104.1 17.1 %all-reduce = (f32[128]{0:T(128)S(1)}, f32[128]{0:T(128)S(1)}, f32[128]{0:T(128)S(1)}) all-reduce(f32[128]{0:T(128)S(1)} %get-tuple-element.6, f32[128]{0:T(128)S(1)} %get-tuple-element.5, f32[128]{0:T(128)S(1)} %get-tuple-element.19), channel_id=1, replica_groups=mesh['groups'=2,'corpus'=8,'retrieve'=2] {'corpus'}, use_global_device_ids=true, to_apply=%region_13.14 | all-reduce | flops 384 | bytes 3072 | tf_op jit(solution)/shard_map/psum | solution.py:25
  121.2 4.1 %multiply_add_fusion = f32[128,768]{1,0:T(8,128)} fusion(f32[128,768]{1,0:T(8,128)S(1)} %get-tuple-element.18, f32[2,128,768]{2,1,0:T(8,128)} %all-reduce.4.cloned.1.call-done, f32[128]{0:T(128)S(1)} %broadcast_divide_fusion, f32[128]{0:T(128)S(1)} %get-tuple-element.13, f32[]{:T(128)} %bitcast.6, f32[128]{0:T(128)S(1)} %broadcast_divide_fusion.1, ...), kind=kLoop, calls=%fused_computation.14 | loop fusion | flops 1376256 | bytes 1575948 | tf_op jit(solution)/shard_map/add | solution.py:73
  125.3 0.0 reduce-scatter.2.cloned.1.call-update
  125.3 6.6 %reduce-scatter.2.cloned.1.call-done = f32[64,768]{1,0:T(8,128)} async-done(((f32[128,768]{1,0:T(8,128)}), f32[64,768]{1,0:T(8,128)}) %reduce-scatter.2.cloned.1.call-update) | async-done | bytes 196624 | tf_op jit(solution)/shard_map/reduce_scatter | solution.py:36
  (4 shorter events, 0.0 us)
Async XLA Ops:
  6.5 51.9 %copy-start = (bf16[768,1792]{1,0:T(8,128)(2,1)S(1)}, bf16[768,1792]{1,0:T(8,128)(2,1)}, u32[]{:S(2)}) copy-start(bf16[768,1792]{1,0:T(8,128)(2,1)} %param.12) | copy-start | bytes 8257540
  6.5 50.3 %all-gather.2.cloned.1.call-start = ((), (), s32[]{:S(2)}) async-start(), calls=%async_computation.1 | async-start | bytes 1843200 | tf_op jit(solution)/shard_map/all_gather | solution.py:45
  8.4 71.4 %all-reduce.4.cloned.1.call-start = ((), (), s32[]{:S(2)}) async-start(), calls=%async_computation.2 | async-start | bytes 1572864 | tf_op jit(solution)/shard_map/psum | solution.py:66
  58.4 3.1 %copy-start.1 = (s32[4]{0:T(128)S(1)}, s32[4]{0:T(128)}, u32[]{:S(2)}) copy-start(s32[4]{0:T(128)} %param.7) | copy-start | bytes 52
  61.5 70.5 %reduce-scatter.2.cloned.1.call-start = ((), (), s32[]{:S(2)}) async-start(), calls=%async_computation.3 | async-start | bytes 589824 | tf_op jit(solution)/shard_map/reduce_scatter | solution.py:36
Sparse Core Ops, SparseCore 0:
  9.5 47.2 all-gather.1
  61.6 18.1 all-reduce.3
  125.4 6.4 reduce-scatter.1
where the time goes:
time: 139 us; the launch traced here: 138 us
  waiting for transfers between devices  66.6 us (48%)
  blocking collectives  38.8 us (28%)
  between operations  13.2 us (9%)
  other arithmetic  10.2 us (7%)
  matrix products  9.05 us (7%)
    all_gather x1, waiting for transfers between devices, body(): piece = lax.all_gather(queries, 'corpus', axis=0, tiled=True)  48.4 us
    pmax x1, blocking collectives, normalise(): lax.pmax((jnp.max(wide_score, axis=1), jnp.max(mid_score, axis=1), jnp.ma...  21.6 us
    psum x1, blocking collectives, normalise(): lax.psum((jnp.sum(powers[0], axis=1), jnp.sum(powers[1], axis=1), jnp.sum...  17.1 us
    psum x1, waiting for transfers between devices, body(): joined = lax.psum(scores[1:], 'retrieve')  11.6 us
    reduce_scatter x1, waiting for transfers between devices, reduce_rows(): return lax.psum_scatter(tile, 'retrieve', scatter_dimension=0, tiled=True)  6.61 us
    dot_general x1, matrix products, body(): jnp.einsum('qd,pd->qp', piece[:, :wide_cols], wide_rows, preferred_elemen...  5.41 us
    add x1, other arithmetic, body(): own_weight * probs[0]  4.05 us
  transfers between devices with their start and end apart: 3, of which 3 were waited for; matrix products, arithmetic and copies ran while one was open for 5% of the time, Pallas kernels for 0%

commit v1 on v0

v1 whole, which is shorter than its diff:
```python
import functools
import math

import jax
import jax.numpy as jnp
from jax import lax
from jax.experimental import pallas as pl
from jax.experimental.pallas import tpu as pltpu
from jax.sharding import PartitionSpec as P

WIDE = 4096
MID = 3584
NARROW = 1024
MESH = pl.DeviceIdType.MESH
LANES = 128
HALF = 64
TILE = 256


def pieces(narrow_cols, mid_cols, wide_cols):
    plan = []
    for which, cols, size in ((2, narrow_cols, 512), (1, mid_cols, 1024), (0, wide_cols, 1024)):
        at = 0
        while at < cols:
            step = min(size, cols - at)
            plan.append((which, at, step))
            at += step
    return plan


def each(count, step):
    if count <= 4:
        for i in range(count):
            step(i)
    else:
        lax.fori_loop(0, count, lambda i, _: (step(i), 0)[1], 0)


def kernel(
    nz, ny, plan,
    w_ref, qw, qm, qn, pw, pm, pn,
    out_ref,
    gw, gm, gn, vw, vm, vn, wide, part, got, tile, mixed, wide_stat, wide_all, mn_all,
    load_sem, pass_sem, send_sem, recv_sem, cross_sem, stat_sem,
):
    nc = nz * ny
    me = lax.axis_index("corpus")
    core = lax.axis_index("retrieve")
    other = 1 - core
    z, y = me // ny, me % ny
    rows = qw.shape[1]
    nq = rows * nc
    half = nq // 2
    nb = half // HALF
    slab = float(pw.shape[1] * nc)
    cols = pw.shape[1]
    own = (qw.at[0], qm, qn)
    full = (gw, gm, gn)
    held = (vw, vm, vn)
    source = (pw.at[0], pm, pn)

    barrier = pltpu.get_barrier_semaphore()

    def greet(j):
        s = lax.rem(me + j + 1, nc)
        for c in range(2):
            pl.semaphore_signal(
                barrier, inc=1, device_id={"corpus": s, "retrieve": c}, device_id_type=MESH
            )

    pl.semaphore_signal(barrier, inc=1, device_id={"retrieve": other}, device_id_type=MESH)
    each(nc - 1, greet)

    def load(i):
        return pltpu.make_async_copy(
            own[i], full[i].at[pl.ds(pl.multiple_of(me * rows, rows), rows)], load_sem.at[i]
        )

    def load_pass(k):
        which, at, step = plan[k]
        return pltpu.make_async_copy(
            source[which].at[:, pl.ds(at, step)],
            held[which].at[:, pl.ds(at, step)],
            pass_sem.at[k],
        )

    for i in range(3):
        load(i).start()
    for k in range(len(plan)):
        load_pass(k).start()

    pl.semaphore_wait(barrier, 2 * nc - 1)

    def block(k, s):
        which, at, step = plan[k]
        return full[which].at[pl.ds(pl.multiple_of(s * rows, rows), rows), pl.ds(at, step)]

    def push(k, s, to, src=None):
        which, at, step = plan[k]
        return pltpu.make_async_remote_copy(
            src_ref=block(k, s) if src is None else src,
            dst_ref=block(k, s),
            send_sem=send_sem.at[which],
            recv_sem=recv_sem.at[k, s],
            device_id={"corpus": to},
            device_id_type=MESH,
        )

    def first(k):
        which, at, step = plan[k]
        mine = own[which].at[:, pl.ds(at, step)]

        def along_y(j):
            push(k, me, z * ny + lax.rem(y + j + 1, ny), mine).start()

        def along_z(j):
            push(k, me, lax.rem(z + j + 1, nz) * ny + y, mine).start()

        each(nz - 1, along_z)
        each(ny - 1, along_y)

    for k in range(len(plan)):
        first(k)
    for i in range(3):
        load(i).wait()

    def forward(k):
        def arrived(j):
            s = lax.rem(z + j + 1, nz) * ny + y
            push(k, s, me).wait_recv()

            def on(i):
                push(k, s, z * ny + lax.rem(y + i + 1, ny)).start()

            each(ny - 1, on)

        each(nz - 1, arrived)

    def collect(k):
        def column(i):
            def row(j):
                s = lax.rem(z + j, nz) * ny + lax.rem(y + i + 1, ny)
                push(k, s, me).wait_recv()

            each(nz, row)

        each(ny - 1, column)

    def multiply(k):
        which, at, step = plan[k]
        load_pass(k).wait()
        into = (wide, part.at[0], part.at[1])[which]

        def product(t, r):
            n0 = pl.ds(pl.multiple_of(t * TILE, TILE), TILE)
            r0 = pl.ds(pl.multiple_of(r * LANES, LANES), LANES)
            value = lax.dot_general(
                full[which][r0, pl.ds(at, step)],
                held[which][n0, pl.ds(at, step)],
                (((1,), (1,)), ((), ())),
                preferred_element_type=jnp.float32,
            )
            if at == 0:
                into[r0, n0] = value
            else:
                into[r0, n0] += value

        each(nq // LANES, lambda r: each(cols // TILE, lambda t: product(t, r)))

    def cross(src, dst, i):
        return pltpu.make_async_remote_copy(
            src_ref=src,
            dst_ref=dst,
            send_sem=cross_sem.at[0, i],
            recv_sem=cross_sem.at[1, i],
            device_id={"retrieve": other},
            device_id_type=MESH,
        )

    def their_rows():
        return pl.ds(pl.multiple_of(other * half, half), half)

    def cross_part(i):
        return cross(part.at[i, their_rows()], got.at[i], i)

    def cross_tile():
        return cross(wide.at[their_rows()], tile, 2)

    def packed(peak, total):
        column = jnp.concatenate([peak, total], axis=0)
        return jnp.broadcast_to(column, (LANES, LANES)).T[0:1]

    def powers(score):
        peak = jnp.max(score, axis=1, keepdims=True)
        power = jnp.exp(score - peak)
        return power, packed(peak, jnp.sum(power, axis=1, keepdims=True))

    def factors(stats, mine, weight):
        top = jnp.max(stats, axis=0)
        grown = jnp.exp(stats - top[None])
        totals = jnp.stack([pltpu.roll(stats[s], HALF, 1) for s in range(stats.shape[0])])
        total = jnp.sum(grown * totals, axis=0)
        factor = jnp.exp(mine - top) * (slab / total) * weight
        return jnp.broadcast_to(factor, (LANES, LANES)).T[:HALF]

    def scaled(power, factor):
        return power * jnp.concatenate([factor] * (cols // LANES), axis=1)

    uniting = [w_ref[i].astype(jnp.float32) * (1.0 / 16.0) for i in range(4)]

    def mn_copy(to):
        return pltpu.make_async_remote_copy(
            src_ref=mn_all.at[me],
            dst_ref=mn_all.at[me],
            send_sem=stat_sem.at[0],
            recv_sem=stat_sem.at[1],
            device_id={"corpus": to},
            device_id_type=MESH,
        )

    def middle_stats():
        for i, width in ((0, MID), (1, NARROW)):
            cross_part(i).wait()
            for b in range(nb):
                rb = pl.ds(pl.multiple_of(core * half + b * HALF, HALF), HALF)
                gb = pl.ds(b * HALF, HALF)
                power, stat = powers((part[i, rb] + got[i, gb]) * (1.0 / math.sqrt(width)))
                got[i, gb] = power
                mn_all[me, i * nb + b] = stat
        each(nc - 1, lambda j: mn_copy(lax.rem(me + j + 1, nc)).start())

    def middle_mix():
        pltpu.make_async_remote_copy(
            src_ref=mn_all.at[pl.ds(0, nc - 1)],
            dst_ref=mn_all.at[pl.ds(0, nc - 1)],
            send_sem=stat_sem.at[0],
            recv_sem=stat_sem.at[1],
            device_id={"corpus": me},
            device_id_type=MESH,
        ).wait()
        for b in range(nb):
            gb = pl.ds(b * HALF, HALF)
            total = None
            for i in range(2):
                at = i * nb + b
                factor = factors(mn_all[:, at], mn_all[me, at], uniting[2 + i])
                term = scaled(got[i, gb], factor)
                total = term if total is None else total + term
            mixed[gb] = total

    def wide_copy(s, c):
        return pltpu.make_async_remote_copy(
            src_ref=wide_stat.at[c],
            dst_ref=wide_all.at[core * nc + me],
            send_sem=stat_sem.at[2],
            recv_sem=stat_sem.at[3],
            device_id={"corpus": s, "retrieve": c},
            device_id_type=MESH,
        )

    def wide_stats():
        for h in range(2):
            for b in range(nb):
                rb = pl.ds(h * half + b * HALF, HALF)
                power, stat = powers(wide[rb] * (1.0 / math.sqrt(WIDE)))
                wide[rb] = power
                wide_stat[h, b] = stat
        wide_all[core * nc + me] = wide_stat[core]

        def tell(j):
            s = lax.rem(me + j + 1, nc)
            for c in range(2):
                wide_copy(s, c).start()

        each(nc - 1, tell)
        wide_copy(me, other).start()
        cross_tile().start()

    def wide_mix():
        pltpu.make_async_remote_copy(
            src_ref=wide_all.at[pl.ds(0, 2 * nc - 1)],
            dst_ref=wide_all.at[pl.ds(0, 2 * nc - 1)],
            send_sem=stat_sem.at[2],
            recv_sem=stat_sem.at[3],
            device_id={"corpus": me},
            device_id_type=MESH,
        ).wait()
        here = [jnp.where(core == 0, uniting[0], uniting[1]), jnp.where(core == 0, uniting[1], uniting[0])]
        spans = []
        for b in range(nb):
            gb = pl.ds(b * HALF, HALF)
            rb = pl.ds(pl.multiple_of(core * half + b * HALF, HALF), HALF)
            mine = factors(wide_all[pl.ds(core * nc, nc), b], wide_all[core * nc + me, b], here[0])
            theirs = factors(wide_all[pl.ds(other * nc, nc), b], wide_all[other * nc + me, b], here[1])
            mixed[gb] += scaled(wide[rb], mine)
            spans.append((gb, theirs))
        cross_tile().wait()
        for gb, theirs in spans:
            out_ref[gb] = mixed[gb] + scaled(tile[gb], theirs)

    last = len(plan) - 1
    narrow_end = max(k for k in range(len(plan)) if plan[k][0] == 2)
    mid_end = max(k for k in range(len(plan)) if plan[k][0] == 1)
    forward(0)
    for k in range(len(plan)):
        if k < last:
            forward(k + 1)
        collect(k)
        multiply(k)
        if k == narrow_end:
            cross_part(1).start()
        if k == mid_end:
            cross_part(0).start()
        if k == mid_end + 1:
            middle_stats()
        if k == last - 1:
            middle_mix()
    wide_stats()
    wide_mix()
    for i in range(3):
        sent = full[i].at[pl.ds(0, (nc - 1) * rows)]
        pltpu.make_async_remote_copy(
            src_ref=sent,
            dst_ref=sent,
            send_sem=send_sem.at[i],
            recv_sem=recv_sem.at[0, 0],
            device_id={"corpus": me},
            device_id_type=MESH,
        ).wait_send()


def body(weights, q_wide, q_mid, q_narrow, pass_wide, pass_mid, pass_narrow):
    nc = lax.axis_size("corpus")
    ny = 1
    while 4 * ny * ny <= nc:
        ny *= 2
    nz = nc // ny
    nq = q_wide.shape[1] * nc
    half = nq // 2
    nb = half // HALF
    cols = pass_wide.shape[1]
    wide_cols, mid_cols, narrow_cols = q_wide.shape[2], q_mid.shape[1], q_narrow.shape[1]
    plan = pieces(narrow_cols, mid_cols, wide_cols)
    f32, bf16 = jnp.float32, jnp.bfloat16
    hbm = pl.BlockSpec(memory_space=pl.ANY)
    features = wide_cols + mid_cols + narrow_cols
    return pl.pallas_call(
        functools.partial(kernel, nz, ny, plan),
        out_shape=jax.ShapeDtypeStruct((half, cols), f32),
        in_specs=[pl.BlockSpec(memory_space=pltpu.SMEM)] + [hbm] * 6,
        out_specs=pl.BlockSpec(memory_space=pltpu.VMEM),
        scratch_shapes=[
            pltpu.VMEM((nq, wide_cols), bf16),
            pltpu.VMEM((nq, mid_cols), bf16),
            pltpu.VMEM((nq, narrow_cols), bf16),
            pltpu.VMEM((cols, wide_cols), bf16),
            pltpu.VMEM((cols, mid_cols), bf16),
            pltpu.VMEM((cols, narrow_cols), bf16),
            pltpu.VMEM((nq, cols), f32),
            pltpu.VMEM((2, nq, cols), f32),
            pltpu.VMEM((2, half, cols), f32),
            pltpu.VMEM((half, cols), f32),
            pltpu.VMEM((half, cols), f32),
            pltpu.VMEM((2, nb, 1, LANES), f32),
            pltpu.VMEM((2 * nc, nb, 1, LANES), f32),
            pltpu.VMEM((nc, 2 * nb, 1, LANES), f32),
            pltpu.SemaphoreType.DMA((3,)),
            pltpu.SemaphoreType.DMA((len(plan),)),
            pltpu.SemaphoreType.DMA((3,)),
            pltpu.SemaphoreType.DMA((len(plan), nc)),
            pltpu.SemaphoreType.DMA((2, 3)),
            pltpu.SemaphoreType.DMA((4,)),
        ],
        compiler_params=pltpu.CompilerParams(
            collective_id=0, has_side_effects=True, vmem_limit_bytes=60 * 1024 * 1024
        ),
        cost_estimate=pl.CostEstimate(
            flops=2 * nq * cols * features,
            bytes_accessed=2 * cols * features,
            transcendentals=2 * nq * cols,
        ),
    )(weights, q_wide, q_mid, q_narrow, pass_wide, pass_mid, pass_narrow)


def solution(mesh):
    return jax.shard_map(
        body,
        mesh=mesh,
        in_specs=(
            P(),
            P("retrieve", ("groups", "corpus"), None),
            P(("groups", "corpus"), "retrieve"),
            P(("groups", "corpus"), "retrieve"),
            P("retrieve", ("groups", "corpus"), None),
            P(("groups", "corpus"), "retrieve"),
            P(("groups", "corpus"), "retrieve"),
        ),
        out_specs=P("retrieve", ("groups", "corpus")),
        check_vma=False,
    )
```

time: 139 us -> 40.2 us (0.29)
  waiting for transfers between devices: 66.6 us -> 0 us
  blocking collectives: 38.8 us -> 0 us
  Pallas kernels: 0 us -> 38.5 us
  between operations: 13.2 us -> 0.01 us
  other arithmetic: 10.2 us -> 0 us
  matrix products: 9.05 us -> 0 us
    all_gather x1 -> x0, waiting for transfers between devices: 48.4 us -> none  [body(): piece = lax.all_gather(queries, 'corpus', axis=0, tiled=True)]
    pallas_call x0 -> x1, Pallas kernels: none -> 38.5 us  [body(): pl.pallas_call(functools.partial(kernel, nz, ny, plan), out_shape=jax.Sha...]
    pmax x1 -> x0, blocking collectives: 21.6 us -> none  [normalise(): lax.pmax((jnp.max(wide_score, axis=1), jnp.max(mid_score, axis=1), jnp.ma...]
    psum x1 -> x0, blocking collectives: 17.1 us -> none  [normalise(): lax.psum((jnp.sum(powers[0], axis=1), jnp.sum(powers[1], axis=1), jnp.sum...]
    psum x1 -> x0, waiting for transfers between devices: 11.6 us -> none  [body(): joined = lax.psum(scores[1:], 'retrieve')]
    dot_general x3 -> x0, matrix products: 9.05 us -> none  [the longest x1 5.41 us: body(): jnp.einsum('qd,pd->qp', piece[:, :wide_cols], wide_rows, preferred_elemen...]
    reduce_scatter x1 -> x0, waiting for transfers between devices: 6.61 us -> none  [reduce_rows(): return lax.psum_scatter(tile, 'retrieve', scatter_dimension=0, tiled=True)]
    add x1 -> x0, other arithmetic: 4.05 us -> none  [body(): own_weight * probs[0]]
  transfers between devices with their start and end apart: 3 -> 0, of which waited for: 3 -> 0; matrix products, arithmetic and copies ran while one was open for 5% -> 0% of each run, Pallas kernels for 0% -> 0%
where the time goes in v1:
time: 40.2 us; the launch traced here: 40.1 us
  Pallas kernels  38.5 us (96%)
  local copies, waits for them, and re-layouts  1.62 us (4%)
    pallas_call x1, Pallas kernels, body(): pl.pallas_call(functools.partial(kernel, nz, ny, plan), out_shape=jax.Sha...  38.5 us
    unnamed x1, local copies, waits for them, and re-layouts  1.62 us

profile of v1, /device:TPU:0, one launch (start us, length us, event | category | flops | bytes accessed | tf_op | source)
XLA Modules:
  0.0 40.1 jit_solution(9295244831014034433)
XLA Ops:
  0.0 38.5 %shard_map.73 = f32[64,768]{1,0:T(8,128)} custom-call(s32[4]{0:T(128)} %w_ref.1, bf16[1,16,4096]{2,1,0:T(8,128)(2,1)} %qw.1, bf16[16,1792]{1,0:T(8,128)(2,1)} %qm.1, bf16[16,512]{1,0:T(8,128)(2,1)} %qn.1, bf16[1,768,4096]{2,1,0:T(8,128)(2,1)} %pw.1, bf16[768,1792]{1,0:T(8,128)(2,1)} %pm.1, bf16[768,512]{1,0:T(8,128)(2,1)} %pn.1), custom_call_target="tpu_custom_call" | custom-call | flops 1258291200 | bytes 9830400 | tf_op jit(solution)/shard_map/pallas_call | solution.py:347
  38.5 1.6 %copy.9 = f32[64,768]{1,0:T(8,128)} copy(f32[64,768]{1,0:T(8,128)} %shard_map.73) | data formatting | bytes 393216

commit v2 on v1

--- a/solution.py
+++ b/solution.py
@@ -61,15 +61,16 @@
 
     barrier = pltpu.get_barrier_semaphore()
 
-    def greet(j):
-        s = lax.rem(me + j + 1, nc)
-        for c in range(2):
-            pl.semaphore_signal(
-                barrier, inc=1, device_id={"corpus": s, "retrieve": c}, device_id_type=MESH
-            )
+    up, down = z + 1 < nz, z > 0
+    neighbours = 1 + (ny - 1) + up.astype(jnp.int32) + down.astype(jnp.int32)
+
+    def greet(s):
+        pl.semaphore_signal(barrier, inc=1, device_id={"corpus": s}, device_id_type=MESH)
 
     pl.semaphore_signal(barrier, inc=1, device_id={"retrieve": other}, device_id_type=MESH)
-    each(nc - 1, greet)
+    each(ny - 1, lambda j: greet(z * ny + lax.rem(y + j + 1, ny)))
+    pl.when(up)(lambda: greet(me + ny))
+    pl.when(down)(lambda: greet(me - ny))
 
     def load(i):
         return pltpu.make_async_copy(
@@ -89,18 +90,18 @@
     for k in range(len(plan)):
         load_pass(k).start()
 
-    pl.semaphore_wait(barrier, 2 * nc - 1)
+    pl.semaphore_wait(barrier, neighbours)
 
     def block(k, s):
         which, at, step = plan[k]
         return full[which].at[pl.ds(pl.multiple_of(s * rows, rows), rows), pl.ds(at, step)]
 
-    def push(k, s, to, src=None):
+    def push(k, s, to, way, src=None):
         which, at, step = plan[k]
         return pltpu.make_async_remote_copy(
             src_ref=block(k, s) if src is None else src,
             dst_ref=block(k, s),
-            send_sem=send_sem.at[which],
+            send_sem=send_sem.at[way, which],
             recv_sem=recv_sem.at[k, s],
             device_id={"corpus": to},
             device_id_type=MESH,
@@ -110,37 +111,27 @@
         which, at, step = plan[k]
         mine = own[which].at[:, pl.ds(at, step)]
 
-        def along_y(j):
-            push(k, me, z * ny + lax.rem(y + j + 1, ny), mine).start()
-
-        def along_z(j):
-            push(k, me, lax.rem(z + j + 1, nz) * ny + y, mine).start()
-
-        each(nz - 1, along_z)
-        each(ny - 1, along_y)
-
-    for k in range(len(plan)):
-        first(k)
+        pl.when(up)(lambda: push(k, me, me + ny, 0, mine).start())
+        pl.when(down)(lambda: push(k, me, me - ny, 1, mine).start())
+        each(ny - 1, lambda j: push(k, me, z * ny + lax.rem(y + j + 1, ny), 2, mine).start())
+
     for i in range(3):
         load(i).wait()
 
-    def forward(k):
-        def arrived(j):
-            s = lax.rem(z + j + 1, nz) * ny + y
-            push(k, s, me).wait_recv()
-
-            def on(i):
-                push(k, s, z * ny + lax.rem(y + i + 1, ny)).start()
-
-            each(ny - 1, on)
-
-        each(nz - 1, arrived)
+    def relay(k, t):
+        def arrived(s, more, ahead, way):
+            push(k, s, me, way).wait_recv()
+            pl.when(more)(lambda: push(k, s, ahead, way).start())
+            each(ny - 1, lambda j: push(k, s, z * ny + lax.rem(y + j + 1, ny), 2).start())
+
+        pl.when(z >= t)(lambda: arrived(me - t * ny, up, me + ny, 0))
+        pl.when(z + t < nz)(lambda: arrived(me + t * ny, down, me - ny, 1))
 
     def collect(k):
         def column(i):
             def row(j):
                 s = lax.rem(z + j, nz) * ny + lax.rem(y + i + 1, ny)
-                push(k, s, me).wait_recv()
+                push(k, s, me, 2).wait_recv()
 
             each(nz, row)
 
@@ -298,35 +289,56 @@
         for gb, theirs in spans:
             out_ref[gb] = mixed[gb] + scaled(tile[gb], theirs)
 
-    last = len(plan) - 1
     narrow_end = max(k for k in range(len(plan)) if plan[k][0] == 2)
     mid_end = max(k for k in range(len(plan)) if plan[k][0] == 1)
-    forward(0)
-    for k in range(len(plan)):
-        if k < last:
-            forward(k + 1)
+    early = range(mid_end + 1)
+    late = range(mid_end + 1, len(plan))
+    cut = mid_end + 1 + len(late) // 2
+    for k in range(cut):
+        first(k)
+    for k in early:
+        relay(k, 1)
+    for k in range(cut, len(plan)):
+        first(k)
+    for t in range(2, nz):
+        for k in early:
+            relay(k, t)
+    for t in range(1, nz):
+        for k in late:
+            relay(k, t)
+        if t == 1:
+            for k in early:
+                collect(k)
+                multiply(k)
+                if k == narrow_end:
+                    cross_part(1).start()
+            cross_part(0).start()
+        if t == 2:
+            middle_stats()
+    for k in late:
         collect(k)
         multiply(k)
-        if k == narrow_end:
-            cross_part(1).start()
-        if k == mid_end:
-            cross_part(0).start()
-        if k == mid_end + 1:
-            middle_stats()
-        if k == last - 1:
+        if k == late[len(late) // 2]:
             middle_mix()
     wide_stats()
     wide_mix()
-    for i in range(3):
-        sent = full[i].at[pl.ds(0, (nc - 1) * rows)]
+
+    def sent(way, i, count):
+        some = full[i].at[pl.ds(0, count * rows)]
         pltpu.make_async_remote_copy(
-            src_ref=sent,
-            dst_ref=sent,
-            send_sem=send_sem.at[i],
+            src_ref=some,
+            dst_ref=some,
+            send_sem=send_sem.at[way, i],
             recv_sem=recv_sem.at[0, 0],
             device_id={"corpus": me},
             device_id_type=MESH,
         ).wait_send()
+
+    for i in range(3):
+        for at in range(nz - 1):
+            pl.when(z == at)(lambda i=i, at=at: sent(0, i, at + 1))
+            pl.when(z == at + 1)(lambda i=i, at=at: sent(1, i, nz - at - 1))
+        sent(2, i, nz * (ny - 1))
 
 
 def body(weights, q_wide, q_mid, q_narrow, pass_wide, pass_mid, pass_narrow):
@@ -366,7 +378,7 @@
             pltpu.VMEM((nc, 2 * nb, 1, LANES), f32),
             pltpu.SemaphoreType.DMA((3,)),
             pltpu.SemaphoreType.DMA((len(plan),)),
-            pltpu.SemaphoreType.DMA((3,)),
+            pltpu.SemaphoreType.DMA((3, 3)),
             pltpu.SemaphoreType.DMA((len(plan), nc)),
             pltpu.SemaphoreType.DMA((2, 3)),
             pltpu.SemaphoreType.DMA((4,)),

time: 40.2 us -> 37.2 us (0.925)
  Pallas kernels: 38.5 us -> 35.4 us
    pallas_call x1, Pallas kernels: 38.5 us -> 35.4 us  [body(): pl.pallas_call(functools.partial(kernel, nz, ny, plan), out_shape=jax.Sha...]
where the time goes in v2:
time: 37.2 us; the launch traced here: 37 us
  Pallas kernels  35.4 us (95%)
  local copies, waits for them, and re-layouts  1.62 us (4%)
    pallas_call x1, Pallas kernels, body(): pl.pallas_call(functools.partial(kernel, nz, ny, plan), out_shape=jax.Sha...  35.4 us
    unnamed x1, local copies, waits for them, and re-layouts  1.62 us

profile of v2, /device:TPU:0, one launch (start us, length us, event | category | flops | bytes accessed | tf_op | source)
XLA Modules:
  0.0 37.0 jit_solution(7571665308407982166)
XLA Ops:
  0.0 35.4 %shard_map.73 = f32[64,768]{1,0:T(8,128)} custom-call(s32[4]{0:T(128)} %w_ref.1, bf16[1,16,4096]{2,1,0:T(8,128)(2,1)} %qw.1, bf16[16,1792]{1,0:T(8,128)(2,1)} %qm.1, bf16[16,512]{1,0:T(8,128)(2,1)} %qn.1, bf16[1,768,4096]{2,1,0:T(8,128)(2,1)} %pw.1, bf16[768,1792]{1,0:T(8,128)(2,1)} %pm.1, bf16[768,512]{1,0:T(8,128)(2,1)} %pn.1), custom_call_target="tpu_custom_call" | custom-call | flops 1258291200 | bytes 9830400 | tf_op jit(solution)/shard_map/pallas_call | solution.py:359
  35.4 1.6 %copy.9 = f32[64,768]{1,0:T(8,128)} copy(f32[64,768]{1,0:T(8,128)} %shard_map.73) | data formatting | bytes 393216

commit v3 on v2

--- a/solution.py
+++ b/solution.py
@@ -87,9 +87,11 @@
 
     for i in range(3):
         load(i).start()
-    for k in range(len(plan)):
+    for k in range(sum(which > 0 for which, _, _ in plan)):
         load_pass(k).start()
 
+    for i in range(3):
+        load(i).wait()
     pl.semaphore_wait(barrier, neighbours)
 
     def block(k, s):
@@ -109,14 +111,12 @@
 
     def first(k):
         which, at, step = plan[k]
-        mine = own[which].at[:, pl.ds(at, step)]
+        mine = None
 
         pl.when(up)(lambda: push(k, me, me + ny, 0, mine).start())
         pl.when(down)(lambda: push(k, me, me - ny, 1, mine).start())
         each(ny - 1, lambda j: push(k, me, z * ny + lax.rem(y + j + 1, ny), 2, mine).start())
 
-    for i in range(3):
-        load(i).wait()
 
     def relay(k, t):
         def arrived(s, more, ahead, way):
@@ -306,6 +306,8 @@
     for t in range(1, nz):
         for k in late:
             relay(k, t)
+            if t == 1:
+                load_pass(k).start()
         if t == 1:
             for k in early:
                 collect(k)

time: 37.2 us -> 35 us (0.941)
  Pallas kernels: 35.4 us -> 33.2 us
    pallas_call x1, Pallas kernels: 35.4 us -> 33.2 us  [body(): pl.pallas_call(functools.partial(kernel, nz, ny, plan), out_shape=jax.Sha...]
where the time goes in v3:
time: 35 us; the launch traced here: 34.8 us
  Pallas kernels  33.2 us (95%)
  local copies, waits for them, and re-layouts  1.62 us (5%)
    pallas_call x1, Pallas kernels, body(): pl.pallas_call(functools.partial(kernel, nz, ny, plan), out_shape=jax.Sha...  33.2 us
    unnamed x1, local copies, waits for them, and re-layouts  1.62 us

profile of v3, /device:TPU:0, one launch (start us, length us, event | category | flops | bytes accessed | tf_op | source)
XLA Modules:
  0.0 34.8 jit_solution(428684994974300118)
XLA Ops:
  0.0 33.2 %shard_map.73 = f32[64,768]{1,0:T(8,128)} custom-call(s32[4]{0:T(128)} %w_ref.1, bf16[1,16,4096]{2,1,0:T(8,128)(2,1)} %qw.1, bf16[16,1792]{1,0:T(8,128)(2,1)} %qm.1, bf16[16,512]{1,0:T(8,128)(2,1)} %qn.1, bf16[1,768,4096]{2,1,0:T(8,128)(2,1)} %pw.1, bf16[768,1792]{1,0:T(8,128)(2,1)} %pm.1, bf16[768,512]{1,0:T(8,128)(2,1)} %pn.1), custom_call_target="tpu_custom_call" | custom-call | flops 1258291200 | bytes 9830400 | tf_op jit(solution)/shard_map/pallas_call | solution.py:361
  33.2 1.6 %copy.9 = f32[64,768]{1,0:T(8,128)} copy(f32[64,768]{1,0:T(8,128)} %shard_map.73) | data formatting | bytes 393216

commit v4 on v3

--- a/solution.py
+++ b/solution.py
@@ -320,9 +320,8 @@
     for k in late:
         collect(k)
         multiply(k)
-        if k == late[len(late) // 2]:
-            middle_mix()
     wide_stats()
+    middle_mix()
     wide_mix()
 
     def sent(way, i, count):

time: 35 us -> 34.8 us (level)
  no operation moved by 1% of the time
where the time goes in v4:
time: 34.8 us; the launch traced here: 34.6 us
  Pallas kernels  33 us (95%)
  local copies, waits for them, and re-layouts  1.62 us (5%)
    pallas_call x1, Pallas kernels, body(): pl.pallas_call(functools.partial(kernel, nz, ny, plan), out_shape=jax.Sha...  33 us
    unnamed x1, local copies, waits for them, and re-layouts  1.62 us

profile of v4, /device:TPU:0, one launch (start us, length us, event | category | flops | bytes accessed | tf_op | source)
XLA Modules:
  0.0 34.6 jit_solution(1357107848155460262)
XLA Ops:
  0.0 33.0 %shard_map.73 = f32[64,768]{1,0:T(8,128)} custom-call(s32[4]{0:T(128)} %w_ref.1, bf16[1,16,4096]{2,1,0:T(8,128)(2,1)} %qw.1, bf16[16,1792]{1,0:T(8,128)(2,1)} %qm.1, bf16[16,512]{1,0:T(8,128)(2,1)} %qn.1, bf16[1,768,4096]{2,1,0:T(8,128)(2,1)} %pw.1, bf16[768,1792]{1,0:T(8,128)(2,1)} %pm.1, bf16[768,512]{1,0:T(8,128)(2,1)} %pn.1), custom_call_target="tpu_custom_call" | custom-call | flops 1258291200 | bytes 9830400 | tf_op jit(solution)/shard_map/pallas_call | solution.py:360
  33.0 1.6 %copy.9 = f32[64,768]{1,0:T(8,128)} copy(f32[64,768]{1,0:T(8,128)} %shard_map.73) | data formatting | bytes 393216
